TPU v7x, 32 devices: a whole 2x2x4 slice. The times are simulated.
32 devices in a mesh: grp: 2 (over x), row: 16 (over z, y, core).
Axes of the slice: x: 2, y: 2, z: 4, core: 2. Of those that a mesh axis runs over, the one named last changes fastest.
Arguments:
- images: bfloat16 [512, 512, 128], P(('grp', 'row')), parts along dimension 0, may hold values from -6 to 6
- weight_one: bfloat16 [3, 3, 128, 256], replicated, may hold values from -0.1875 to 0.1875
- bias_one: float32 [256], replicated, may hold values from -3 to 3
- weight_two: bfloat16 [3, 3, 256, 256], replicated, may hold values from -0.125 to 0.125
- bias_two: float32 [256], replicated, may hold values from -3 to 3
- cotangent: bfloat16 [256, 256, 256], P(('grp', 'row')), parts along dimension 0, may hold values from -0.0234375 to 0.0234375
Outputs:
- coarse_out: bfloat16 [256, 256, 256], P(('grp', 'row')), parts along dimension 0
- grad_w_one: float32 [6, 3, 128, 256], P('grp'), parts along dimension 0
- grad_b_one: float32 [512], P('grp'), parts along dimension 0
- grad_w_two: float32 [6, 3, 256, 256], P('grp'), parts along dimension 0
- grad_b_two: float32 [512], P('grp'), parts along dimension 0
There are 2 independent parts, one for each index of `grp`. A program takes and returns all parts, laid end to end along the dimension named above; an argument that names none is the same for every part. Nothing has to cross between parts.
All inputs are finite; a program needn't handle non-finite values.
Results may differ from a plain program's by a relative error of at most 0.0044.
Values may be sent and summed in bfloat16 or wider, within the bound.
A program may use at most 64 MiB of HBM per device.

v0:
```python
import functools

import jax
import jax.numpy as jnp
from jax import lax
from jax.experimental import pallas as pl
from jax.experimental.pallas import tpu as pltpu
from jax.sharding import PartitionSpec as P

BF = jnp.bfloat16
F32 = jnp.float32
MESH = pl.DeviceIdType.MESH


def plan(total, order):
    levels, size, offset = [], total, 0
    for distance in order:
        halves = (size // 2) % 16 == 0
        if halves:
            size //= 2
        levels.append((distance, size, halves, offset))
        offset += size
    return levels, offset


def order_of(count):
    near = []
    distance = 1
    while distance < count:
        near.append(distance)
        distance *= 2
    return near, near[:1] + near[2:] + near[1:2]


def remote(src, dst, send, recv, to):
    return pltpu.make_async_remote_copy(
        src_ref=src, dst_ref=dst, send_sem=send, recv_sem=recv, device_id={"row": to}, device_id_type=MESH
    )


class Sum:
    def __init__(self, me, levels, acc, sent, got, full, rs_sems, ag_sems):
        self.me, self.levels = me, levels
        self.acc, self.sent, self.got, self.full = acc, sent, got, full
        self.rs_sems, self.ag_sems = rs_sems, ag_sems
        self.base, self.at = 0, 0
        self.copies, self.keep = [], None
        self.gathers = [i for i, level in enumerate(levels) if level[2]][::-1]

    def rows(self, base, size):
        return pl.ds(base if isinstance(base, int) else pl.multiple_of(base, 16), size)

    def bit(self, level):
        return lax.rem(lax.div(self.me, level[0]), 2)

    def partner(self, level):
        return self.me + level[0] * (1 - 2 * self.bit(level))

    def start(self):
        i = self.at
        level = self.levels[i]
        _, size, halves, offset = level
        bit = self.bit(level)
        own = self.rows(offset, size)
        out = self.base + (1 - bit) * size if halves else self.base
        self.keep = self.base + bit * size if halves else self.base
        self.sent[own] = self.acc[self.rows(out, size)].astype(BF)
        copy = remote(self.sent.at[own], self.got.at[own], self.rs_sems.at[0, i], self.rs_sems.at[1, i], self.partner(level))
        copy.start()
        self.copies.append(copy)

    def finish(self):
        i = self.at
        _, size, halves, offset = self.levels[i]
        self.copies[i].wait()
        own = self.rows(offset, size)
        kept = self.rows(self.keep, size)
        mine = self.acc[kept] if halves else self.sent[own].astype(F32)
        total = mine + self.got[own].astype(F32)
        self.base = self.keep
        self.at += 1
        if self.at == len(self.levels):
            self.full[kept] = total.astype(BF)
            self.gather()
        else:
            self.acc[kept] = total
            self.start()

    def gather(self):
        k = self.at - len(self.levels)
        level = self.levels[self.gathers[k]]
        block = self.full.at[self.rows(self.base, level[1])]
        copy = remote(block, block, self.ag_sems.at[0, k], self.ag_sems.at[1, k], self.partner(level))
        copy.start()
        self.copies.append(copy)

    def gathered(self):
        k = self.at - len(self.levels)
        level = self.levels[self.gathers[k]]
        self.copies[self.at].wait()
        self.base = self.base - self.bit(level) * level[1]
        self.at += 1
        if k + 1 < len(self.gathers):
            self.gather()

    def done(self):
        return self.at == len(self.levels) + len(self.gathers)

    def step(self):
        if self.at < len(self.levels):
            self.finish()
        elif not self.done():
            self.gathered()


def shifted(x):
    wide = x.astype(F32)
    count = x.shape[0]
    row = lax.broadcasted_iota(jnp.int32, x.shape, 0)
    down = jnp.where(row == 0, 0.0, pltpu.roll(wide, 1, 0))
    up = jnp.where(row == count - 1, 0.0, pltpu.roll(wide, count - 1, 0))
    return down.astype(BF), up.astype(BF)


def dot(a, b):
    return jnp.dot(a, b, preferred_element_type=F32)


def kernel(
    count, levels_two, levels_one,
    img_h, w1_h, b1, w2_h, b2, cot_h,
    out, gw1, gw2,
    img, cot, w1, w2, w2t, wide, eo_even, eo_odd, os_even, os_odd,
    himg, hcot, hhid, c3, h3, pre, ht, gt,
    acc2, sent2, got2, full2, acc1, sent1, got1, full1,
    local_sems, halo_sems, rs2, ag2, rs1, ag1,
):
    me = lax.axis_index("row")
    rows, cols = cot_h.shape[0], cot_h.shape[1]
    has_up, has_down = me > 0, me < count - 1
    partners = [me + lv[0] * (1 - 2 * lax.rem(lax.div(me, lv[0]), 2)) for lv in levels_two]

    loads = [
        pltpu.make_async_copy(img_h, img, local_sems.at[0]),
        pltpu.make_async_copy(cot_h, cot, local_sems.at[1]),
        pltpu.make_async_copy(w1_h.at[0, pl.ds(1, 2)], w1.at[pl.ds(0, 2)], local_sems.at[2]),
        pltpu.make_async_copy(w1_h.at[1, pl.ds(1, 2)], w1.at[pl.ds(2, 2)], local_sems.at[3]),
        pltpu.make_async_copy(w1_h.at[2, pl.ds(1, 2)], w1.at[pl.ds(4, 2)], local_sems.at[4]),
        pltpu.make_async_copy(w1_h.at[pl.ds(0, 3), 0], w1.at[pl.ds(6, 3)], local_sems.at[5]),
        pltpu.make_async_copy(w2_h, w2, local_sems.at[6]),
    ]
    for load in loads:
        load.start()

    barrier = pltpu.get_barrier_semaphore()
    for partner in partners:
        pl.semaphore_signal(barrier, inc=1, device_id={"row": partner}, device_id_type=MESH)

    @pl.when(has_up)
    def _():
        pl.semaphore_signal(barrier, inc=1, device_id={"row": me - 1}, device_id_type=MESH)

    @pl.when(has_down)
    def _():
        pl.semaphore_signal(barrier, inc=1, device_id={"row": me + 1}, device_id_type=MESH)

    pl.semaphore_wait(barrier, len(partners) + has_up.astype(jnp.int32) + has_down.astype(jnp.int32))

    down_img = remote(img_h.at[img_h.shape[0] - 1], himg, halo_sems.at[0, 0], halo_sems.at[1, 0], me + 1)
    down_cot = remote(cot_h.at[rows - 1], hcot.at[0], halo_sems.at[0, 1], halo_sems.at[1, 1], me + 1)
    up_cot = remote(cot_h.at[0], hcot.at[1], halo_sems.at[0, 2], halo_sems.at[1, 2], me - 1)
    down_hid = remote(h3.at[rows, :, pl.ds(256, 256)], hhid.at[0], halo_sems.at[0, 3], halo_sems.at[1, 3], me + 1)
    up_hid = remote(h3.at[1, :, pl.ds(256, 256)], hhid.at[1], halo_sems.at[0, 4], halo_sems.at[1, 4], me - 1)

    @pl.when(has_down)
    def _():
        down_img.start()
        down_cot.start()

    @pl.when(has_up)
    def _():
        up_cot.start()

    wide[pl.ds(0, 8)] = jnp.zeros((8, wide.shape[1]), F32)

    def split(x, eo, os, at):
        wide[pl.ds(8, 2 * cols)] = x.astype(F32)
        eo[at, :, pl.ds(0, 128)] = wide[pl.ds(8, cols, stride=2)].astype(BF)
        eo[at, :, pl.ds(128, 128)] = wide[pl.ds(9, cols, stride=2)].astype(BF)
        os[at] = wide[pl.ds(7, cols, stride=2)].astype(BF)

    loads[0].wait()

    def split_pair(o, carry):
        split(img[2 * o], eo_odd, os_odd, o)
        split(img[2 * o + 1], eo_even, os_even, o + 1)
        return carry

    lax.fori_loop(0, rows, split_pair, 0)

    @pl.when(jnp.logical_not(has_up))
    def _():
        himg[...] = jnp.zeros_like(himg)
        hcot[0] = jnp.zeros(hcot.shape[1:], BF)
        hhid[0] = jnp.zeros(hhid.shape[1:], BF)

    @pl.when(jnp.logical_not(has_down))
    def _():
        hcot[1] = jnp.zeros(hcot.shape[1:], BF)
        hhid[1] = jnp.zeros(hhid.shape[1:], BF)

    def put(ref, at, x, flip):
        down, up = shifted(x)
        ref[at, :, pl.ds(0, 256)] = up if flip else down
        ref[at, :, pl.ds(256, 256)] = x
        ref[at, :, pl.ds(512, 256)] = down if flip else up

    loads[1].wait()

    def place_cot(o, carry):
        put(c3, o + 1, cot[o], True)
        return carry

    lax.fori_loop(0, rows, place_cot, 0)
    for load in loads[2:]:
        load.wait()
    for tap in range(9):
        w2t[tap] = w2[tap // 3, tap % 3].T

    @pl.when(has_up)
    def _():
        down_img.wait_recv()
        down_cot.wait_recv()

    @pl.when(has_down)
    def _():
        up_cot.wait_recv()

    split(himg[...], eo_even, os_even, 0)
    put(c3, 0, hcot[0], True)
    put(c3, rows + 1, hcot[1], True)

    block = 2
    size = block * cols

    def flat(ref, at, n=block):
        return ref[pl.ds(at, n)].reshape(n * cols, ref.shape[2])

    def conv_one(i, carry):
        o = i * block
        taps = jnp.concatenate(
            [flat(eo_even, o), flat(eo_odd, o), flat(eo_even, o + 1), flat(os_even, o), flat(os_odd, o), flat(os_even, o + 1)],
            axis=1,
        )
        result = dot(taps, w1[...].reshape(-1, 256)) + b1[...]
        pre[pl.ds(pl.multiple_of(o * cols, size), size)] = result
        hidden = jnp.maximum(result, 0.0).astype(BF)
        for k in range(block):
            one = hidden[k * cols:(k + 1) * cols]
            put(h3, o + k + 1, one, False)
            ht[o + k] = one.T
        return carry

    lax.fori_loop(0, rows // block, conv_one, 0)

    @pl.when(has_down)
    def _():
        down_hid.start()

    @pl.when(has_up)
    def _():
        up_hid.start()

    hidden_t = jnp.concatenate([ht[o] for o in range(rows)], axis=1)
    for a in range(3):
        result = dot(hidden_t, flat(c3, 2 - a, rows))
        for b in range(3):
            acc2[pl.ds((a * 3 + b) * 256, 256)] = result[:, b * 256:(b + 1) * 256]
    two = Sum(me, levels_two, acc2, sent2, got2, full2, rs2, ag2)
    two.start()

    def grad_hidden(i, carry):
        o = i * block
        taps = jnp.concatenate([flat(c3, o + 2), flat(c3, o + 1), flat(c3, o)], axis=1)
        grad = dot(taps, w2t[...].reshape(-1, 256))
        grad = jnp.where(pre[pl.ds(pl.multiple_of(o * cols, size), size)] > 0.0, grad, 0.0).astype(BF)
        for k in range(block):
            gt[o + k] = grad[k * cols:(k + 1) * cols].T
        return carry

    half = rows // block // 2
    lax.fori_loop(0, half, grad_hidden, 0)
    two.step()
    lax.fori_loop(half, rows // block, grad_hidden, 0)

    grad_t = jnp.concatenate([gt[o] for o in range(rows)], axis=1)
    eos = [flat(eo_even, 0, rows), flat(eo_odd, 0, rows), flat(eo_even, 1, rows)]
    for a in range(3):
        acc1[pl.ds((a * 3 + 1) * 128, 256)] = dot(grad_t, eos[a]).T
    ones = jnp.ones((rows * cols, 128), BF)
    last = dot(grad_t, jnp.concatenate([flat(os_even, 0, rows), flat(os_odd, 0, rows), flat(os_even, 1, rows), ones], axis=1)).T
    for a in range(3):
        acc1[pl.ds(a * 384, 128)] = last[a * 128:(a + 1) * 128]
    acc1[pl.ds(1152, 64)] = last[384:448]
    total = jnp.sum(cot[...].reshape(rows * cols, 256).astype(F32), axis=0, keepdims=True)
    acc1[pl.ds(1216, 64)] = jnp.broadcast_to(total, (64, 256))
    one = Sum(me, levels_one, acc1, sent1, got1, full1, rs1, ag1)
    one.start()

    @pl.when(has_up)
    def _():
        down_hid.wait_recv()

    @pl.when(has_down)
    def _():
        up_hid.wait_recv()

    put(h3, 0, hhid[0], False)
    put(h3, rows + 1, hhid[1], False)

    def conv_two(i, carry):
        o = i * block
        taps = jnp.concatenate([flat(h3, o), flat(h3, o + 1), flat(h3, o + 2)], axis=1)
        result = dot(taps, w2[...].reshape(-1, 256)) + b2[...]
        out[pl.ds(o, block)] = result.astype(BF).reshape(block, cols, 256)
        return carry

    lax.fori_loop(0, half, conv_two, 0)
    two.step()
    one.step()
    lax.fori_loop(half, rows // block, conv_two, 0)

    while not (one.done() and two.done()):
        one.step()
        two.step()
    gw1[...] = full1[...]
    gw2[...] = full2[...]

    @pl.when(has_down)
    def _():
        down_img.wait_send()
        down_cot.wait_send()
        down_hid.wait_send()

    @pl.when(has_up)
    def _():
        up_cot.wait_send()
        up_hid.wait_send()


def local(count, images, weight_one, bias_one, weight_two, bias_two, cotangent):
    rows, cols, depth = cotangent.shape
    order_two, order_one = order_of(count)
    levels_two, span_two = plan(9 * depth, order_two)
    levels_one, span_one = plan(9 * images.shape[2] + 128, order_one)
    vmem = pl.BlockSpec(memory_space=pltpu.VMEM)
    hbm = pl.BlockSpec(memory_space=pl.ANY)
    n = len(order_two)
    size_one, size_two = 9 * 128 + 128, 9 * 256
    out, gw1, gw2 = pl.pallas_call(
        functools.partial(kernel, count, levels_two, levels_one),
        out_shape=(
            jax.ShapeDtypeStruct(cotangent.shape, BF),
            jax.ShapeDtypeStruct((size_one, 256), BF),
            jax.ShapeDtypeStruct((size_two, 256), BF),
        ),
        in_specs=[hbm, hbm, vmem, hbm, vmem, hbm],
        out_specs=(vmem, vmem, vmem),
        scratch_shapes=[
            pltpu.VMEM(images.shape, BF),
            pltpu.VMEM(cotangent.shape, BF),
            pltpu.VMEM((9, 128, 256), BF),
            pltpu.VMEM((3, 3, 256, 256), BF),
            pltpu.VMEM((9, 256, 256), BF),
            pltpu.VMEM((2 * cols + 8, 128), F32),
            pltpu.VMEM((rows + 1, cols, 256), BF),
            pltpu.VMEM((rows, cols, 256), BF),
            pltpu.VMEM((rows + 1, cols, 128), BF),
            pltpu.VMEM((rows, cols, 128), BF),
            pltpu.VMEM(images.shape[1:], BF),
            pltpu.VMEM((2, cols, 256), BF),
            pltpu.VMEM((2, cols, 256), BF),
            pltpu.VMEM((rows + 2, cols, 768), BF),
            pltpu.VMEM((rows + 2, cols, 768), BF),
            pltpu.VMEM((rows * cols, 256), F32),
            pltpu.VMEM((rows, 256, cols), BF),
            pltpu.VMEM((rows, 256, cols), BF),
            pltpu.VMEM((size_two, 256), F32),
            pltpu.VMEM((span_two, 256), BF),
            pltpu.VMEM((span_two, 256), BF),
            pltpu.VMEM((size_two, 256), BF),
            pltpu.VMEM((size_one, 256), F32),
            pltpu.VMEM((span_one, 256), BF),
            pltpu.VMEM((span_one, 256), BF),
            pltpu.VMEM((size_one, 256), BF),
            pltpu.SemaphoreType.DMA((7,)),
            pltpu.SemaphoreType.DMA((2, 5)),
            pltpu.SemaphoreType.DMA((2, n)),
            pltpu.SemaphoreType.DMA((2, n)),
            pltpu.SemaphoreType.DMA((2, n)),
            pltpu.SemaphoreType.DMA((2, n)),
        ],
        compiler_params=pltpu.CompilerParams(
            collective_id=0, has_side_effects=True, vmem_limit_bytes=56 * 1024 * 1024
        ),
    )(images, weight_one, bias_one[None], weight_two, bias_two[None], cotangent)
    grads_one = gw1.astype(F32)
    return (
        out,
        grads_one[:1152].reshape(3, 3, 128, 256),
        grads_one[1152],
        gw2.astype(F32).reshape(3, 3, 256, 256),
        grads_one[1216],
    )


def solution(mesh):
    placed = (P(("grp", "row"), None, None), P(), P(), P(), P(), P(("grp", "row"), None, None))
    return jax.shard_map(
        functools.partial(local, mesh.shape["row"]),
        mesh=mesh,
        in_specs=placed,
        out_specs=(
            P(("grp", "row"), None, None),
            P("grp", None, None, None),
            P("grp"),
            P("grp", None, None, None),
            P("grp"),
        ),
        check_vma=False,
    )
```

profile of v0, /device:TPU:0, one launch (start us, length us, event | category | flops | bytes accessed | tf_op | source)
XLA Modules:
  0.0 69.9 jit_solution(18047457168385260713)
XLA Ops:
  0.6 63.1 %shard_map.101 = (bf16[8,256,256]{2,1,0:T(8,128)(2,1)}, bf16[1280,256]{1,0:T(8,128)(2,1)}, bf16[2304,256]{1,0:T(8,128)(2,1)}) custom-call(bf16[16,512,128]{2,1,0:T(8,128)(2,1)} %img_h.1, bf16[3,3,128,256]{3,2,1,0:T(8,128)(2,1)} %w1_h.1, f32[1,256]{1,0:T(1,128)} %bitcast.9, bf16[3,3,256,256]{3,2,1,0:T(8,128)(2,1)} %w2_h.1, f32[1,256]{1,0:T(1,128)} %bitcast.10, ...), custom_call_target="tpu_custom_call" | custom-call | tf_op jit(solution)/shard_map/pallas_call | solution.py:360
  63.8 1.3 %fusion = (f32[1,256]{1,0:T(1,128)}, f32[1,256]{1,0:T(1,128)}) fusion(bf16[1280,256]{1,0:T(8,128)(2,1)} %get-tuple-element.9), kind=kLoop, calls=%fused_computation | loop fusion | bytes 4096 | tf_op jit(solution)/shard_map/slice | solution.py:413
  65.0 0.0 copy-start
  65.0 2.3 %slice.12 = f32[1152,256]{1,0:T(8,128)} slice(bf16[1280,256]{1,0:T(8,128)(2,1)} %get-tuple-element.9), slice={[0:1152], [0:256]} | slice | bytes 2359296 | tf_op jit(solution)/shard_map/slice | solution.py:410
  67.3 0.0 copy-done
  67.3 0.0 copy-start.1
  67.3 1.6 %convert.1 = f32[3,3,256,256]{3,2,1,0:T(8,128)} convert(bf16[3,3,256,256]{3,2,1,0:T(8,128)(2,1)S(1)} %bitcast.7) | non-fusion elementwise | flops 589824 | bytes 3538944 | tf_op jit(solution)/shard_map/reshape | solution.py:412
  68.9 0.0 copy-done.1
  68.9 1.0 %copy.12 = bf16[8,256,256]{2,1,0:T(8,128)(2,1)} copy(bf16[8,256,256]{2,1,0:T(8,128)(2,1)S(1)} %copy-done.1) | data formatting | bytes 2097152
Async XLA Ops:
  65.0 2.3 %copy-start = (bf16[2304,256]{1,0:T(8,128)(2,1)S(1)}, bf16[2304,256]{1,0:T(8,128)(2,1)}, u32[]{:S(2)}) copy-start(bf16[2304,256]{1,0:T(8,128)(2,1)} %get-tuple-element.10) | copy-start | bytes 3538948
  67.3 1.6 %copy-start.1 = (bf16[8,256,256]{2,1,0:T(8,128)(2,1)S(1)}, bf16[8,256,256]{2,1,0:T(8,128)(2,1)}, u32[]{:S(2)}) copy-start(bf16[8,256,256]{2,1,0:T(8,128)(2,1)} %get-tuple-element.18) | copy-start | bytes 3145732
where the time goes:
time: 70.2 us; the launch traced here: 69.9 us
  Pallas kernels  63.1 us (90%)
  local copies, waits for them, and re-layouts  4.49 us (6%)
  other arithmetic  1.63 us (2%)
    pallas_call x1, Pallas kernels, local(): pl.pallas_call(functools.partial(kernel, count, levels_two, levels_one),...  63.1 us
    slice x1, local copies, waits for them, and re-layouts, local(): grads_one[:1152].reshape(3, 3, 128, 256)  2.26 us
    reshape x1, other arithmetic, local(): gw2.astype(F32).reshape(3, 3, 256, 256)  1.63 us

commit v1 on v0

--- a/solution.py
+++ b/solution.py
@@ -15,7 +15,7 @@
 def plan(total, order):
     levels, size, offset = [], total, 0
     for distance in order:
-        halves = (size // 2) % 16 == 0
+        halves = (size // 2) % 16 == 0 and distance != order[-1]
         if halves:
             size //= 2
         levels.append((distance, size, halves, offset))
@@ -39,7 +39,8 @@
 
 
 class Sum:
-    def __init__(self, me, levels, acc, sent, got, full, rs_sems, ag_sems):
+    def __init__(self, me, levels, refs):
+        acc, sent, got, full, rs_sems, ag_sems = refs
         self.me, self.levels = me, levels
         self.acc, self.sent, self.got, self.full = acc, sent, got, full
         self.rs_sems, self.ag_sems = rs_sems, ag_sems
@@ -64,7 +65,7 @@
         own = self.rows(offset, size)
         out = self.base + (1 - bit) * size if halves else self.base
         self.keep = self.base + bit * size if halves else self.base
-        self.sent[own] = self.acc[self.rows(out, size)].astype(BF)
+        self.sent[own] = self.acc[self.rows(out, size)].astype(self.sent.dtype)
         copy = remote(self.sent.at[own], self.got.at[own], self.rs_sems.at[0, i], self.rs_sems.at[1, i], self.partner(level))
         copy.start()
         self.copies.append(copy)
@@ -80,8 +81,9 @@
         self.base = self.keep
         self.at += 1
         if self.at == len(self.levels):
-            self.full[kept] = total.astype(BF)
-            self.gather()
+            self.full[kept] = total.astype(self.full.dtype)
+            if self.gathers:
+                self.gather()
         else:
             self.acc[kept] = total
             self.start()
@@ -127,18 +129,18 @@
 
 
 def kernel(
-    count, levels_two, levels_one,
+    count, plans,
     img_h, w1_h, b1, w2_h, b2, cot_h,
-    out, gw1, gw2,
-    img, cot, w1, w2, w2t, wide, eo_even, eo_odd, os_even, os_odd,
+    out_h, gw1_h, gw2_h, biases,
+    out, img, cot, w1, w2, w2t, wide, eo_even, eo_odd, os_even, os_odd,
     himg, hcot, hhid, c3, h3, pre, ht, gt,
-    acc2, sent2, got2, full2, acc1, sent1, got1, full1,
-    local_sems, halo_sems, rs2, ag2, rs1, ag1,
+    local_sems, halo_sems, out_sems, *stream_refs,
 ):
     me = lax.axis_index("row")
     rows, cols = cot_h.shape[0], cot_h.shape[1]
     has_up, has_down = me > 0, me < count - 1
-    partners = [me + lv[0] * (1 - 2 * lax.rem(lax.div(me, lv[0]), 2)) for lv in levels_two]
+    partners = [me + lv[0] * (1 - 2 * lax.rem(lax.div(me, lv[0]), 2)) for lv in plans[0]]
+    streams = [Sum(me, levels, stream_refs[6 * k:6 * k + 6]) for k, levels in enumerate(plans)]
 
     loads = [
         pltpu.make_async_copy(img_h, img, local_sems.at[0]),
@@ -226,19 +228,6 @@
         load.wait()
     for tap in range(9):
         w2t[tap] = w2[tap // 3, tap % 3].T
-
-    @pl.when(has_up)
-    def _():
-        down_img.wait_recv()
-        down_cot.wait_recv()
-
-    @pl.when(has_down)
-    def _():
-        up_cot.wait_recv()
-
-    split(himg[...], eo_even, os_even, 0)
-    put(c3, 0, hcot[0], True)
-    put(c3, rows + 1, hcot[1], True)
 
     block = 2
     size = block * cols
@@ -261,24 +250,6 @@
             ht[o + k] = one.T
         return carry
 
-    lax.fori_loop(0, rows // block, conv_one, 0)
-
-    @pl.when(has_down)
-    def _():
-        down_hid.start()
-
-    @pl.when(has_up)
-    def _():
-        up_hid.start()
-
-    hidden_t = jnp.concatenate([ht[o] for o in range(rows)], axis=1)
-    for a in range(3):
-        result = dot(hidden_t, flat(c3, 2 - a, rows))
-        for b in range(3):
-            acc2[pl.ds((a * 3 + b) * 256, 256)] = result[:, b * 256:(b + 1) * 256]
-    two = Sum(me, levels_two, acc2, sent2, got2, full2, rs2, ag2)
-    two.start()
-
     def grad_hidden(i, carry):
         o = i * block
         taps = jnp.concatenate([flat(c3, o + 2), flat(c3, o + 1), flat(c3, o)], axis=1)
@@ -288,24 +259,80 @@
             gt[o + k] = grad[k * cols:(k + 1) * cols].T
         return carry
 
-    half = rows // block // 2
-    lax.fori_loop(0, half, grad_hidden, 0)
-    two.step()
-    lax.fori_loop(half, rows // block, grad_hidden, 0)
+    def conv_two(i, carry):
+        o = i * block
+        taps = jnp.concatenate([flat(h3, o), flat(h3, o + 1), flat(h3, o + 2)], axis=1)
+        result = dot(taps, w2[...].reshape(-1, 256)) + b2[...]
+        out[pl.ds(o, block)] = result.astype(BF).reshape(block, cols, 256)
+        return carry
+
+    blocks = rows // block
+
+    def work(first, last, body):
+        lax.fori_loop(first, last, body, 0)
+
+    work(1, blocks, conv_one)
+    work(1, blocks - 1, grad_hidden)
+
+    @pl.when(has_up)
+    def _():
+        down_img.wait_recv()
+
+    split(himg[...], eo_even, os_even, 0)
+    work(0, 1, conv_one)
+
+    @pl.when(has_down)
+    def _():
+        down_hid.start()
+
+    @pl.when(has_up)
+    def _():
+        up_hid.start()
+
+    hidden_t = jnp.concatenate([ht[o] for o in range(rows)], axis=1)
+
+    def taps_two(a):
+        result = dot(hidden_t, flat(c3, 2 - a, rows))
+        for b in range(3):
+            streams[a].acc[pl.ds(b * 256, 256)] = result[:, b * 256:(b + 1) * 256]
+        streams[a].start()
+
+    taps_two(1)
+
+    @pl.when(has_up)
+    def _():
+        down_cot.wait_recv()
+
+    put(c3, 0, hcot[0], True)
+    taps_two(2)
+
+    @pl.when(has_down)
+    def _():
+        up_cot.wait_recv()
+
+    put(c3, rows + 1, hcot[1], True)
+    streams[1].step()
+    taps_two(0)
+    work(0, 1, grad_hidden)
+    streams[2].step()
+    work(blocks - 1, blocks, grad_hidden)
+    streams[0].step()
 
     grad_t = jnp.concatenate([gt[o] for o in range(rows)], axis=1)
     eos = [flat(eo_even, 0, rows), flat(eo_odd, 0, rows), flat(eo_even, 1, rows)]
+    acc1 = streams[3].acc
     for a in range(3):
         acc1[pl.ds((a * 3 + 1) * 128, 256)] = dot(grad_t, eos[a]).T
     ones = jnp.ones((rows * cols, 128), BF)
     last = dot(grad_t, jnp.concatenate([flat(os_even, 0, rows), flat(os_odd, 0, rows), flat(os_even, 1, rows), ones], axis=1)).T
     for a in range(3):
         acc1[pl.ds(a * 384, 128)] = last[a * 128:(a + 1) * 128]
-    acc1[pl.ds(1152, 64)] = last[384:448]
+    streams[3].start()
+    streams[1].step()
+    streams[4].acc[pl.ds(0, 8)] = last[384:392]
     total = jnp.sum(cot[...].reshape(rows * cols, 256).astype(F32), axis=0, keepdims=True)
-    acc1[pl.ds(1216, 64)] = jnp.broadcast_to(total, (64, 256))
-    one = Sum(me, levels_one, acc1, sent1, got1, full1, rs1, ag1)
-    one.start()
+    streams[4].acc[pl.ds(8, 8)] = jnp.broadcast_to(total, (8, 256))
+    streams[4].start()
 
     @pl.when(has_up)
     def _():
@@ -317,24 +344,32 @@
 
     put(h3, 0, hhid[0], False)
     put(h3, rows + 1, hhid[1], False)
-
-    def conv_two(i, carry):
-        o = i * block
-        taps = jnp.concatenate([flat(h3, o), flat(h3, o + 1), flat(h3, o + 2)], axis=1)
-        result = dot(taps, w2[...].reshape(-1, 256)) + b2[...]
-        out[pl.ds(o, block)] = result.astype(BF).reshape(block, cols, 256)
-        return carry
-
-    lax.fori_loop(0, half, conv_two, 0)
-    two.step()
-    one.step()
-    lax.fori_loop(half, rows // block, conv_two, 0)
-
-    while not (one.done() and two.done()):
-        one.step()
-        two.step()
-    gw1[...] = full1[...]
-    gw2[...] = full2[...]
+    work(0, 1, conv_two)
+    streams[2].step()
+    streams[3].step()
+    work(1, 2, conv_two)
+    streams[1].step()
+    streams[0].step()
+    streams[4].step()
+    work(2, 3, conv_two)
+    streams[2].step()
+    work(3, blocks, conv_two)
+
+    results = [gw2_h.at[pl.ds(a * 768, 768)] for a in range(3)] + [gw1_h]
+    stores = [pltpu.make_async_copy(out, out_h, out_sems.at[4])]
+    stores[0].start()
+    stored = set()
+    while len(stored) < 5:
+        for k in (1, 2, 0, 3, 4):
+            streams[k].step()
+            if streams[k].done() and k not in stored:
+                stored.add(k)
+                if k < 4:
+                    stores.append(pltpu.make_async_copy(streams[k].full, results[k], out_sems.at[k]))
+                    stores[-1].start()
+    biases[...] = streams[4].full[...]
+    for store in stores:
+        store.wait()
 
     @pl.when(has_down)
     def _():
@@ -350,23 +385,36 @@
 
 def local(count, images, weight_one, bias_one, weight_two, bias_two, cotangent):
     rows, cols, depth = cotangent.shape
-    order_two, order_one = order_of(count)
-    levels_two, span_two = plan(9 * depth, order_two)
-    levels_one, span_one = plan(9 * images.shape[2] + 128, order_one)
+    y_first, z_first = order_of(count)
+    totals = (768, 768, 768, 1152, 16)
+    planned = [plan(size, z_first if k == 1 else y_first) for k, size in enumerate(totals)]
+    n = len(y_first)
+    stream_shapes = []
+    for k, (size, (_, span)) in enumerate(zip(totals, planned)):
+        kind = F32 if k == 4 else BF
+        stream_shapes += [
+            pltpu.VMEM((size, 256), F32),
+            pltpu.VMEM((span, 256), kind),
+            pltpu.VMEM((span, 256), kind),
+            pltpu.VMEM((size, 256), kind),
+            pltpu.SemaphoreType.DMA((2, n)),
+            pltpu.SemaphoreType.DMA((2, n)),
+        ]
     vmem = pl.BlockSpec(memory_space=pltpu.VMEM)
     hbm = pl.BlockSpec(memory_space=pl.ANY)
-    n = len(order_two)
-    size_one, size_two = 9 * 128 + 128, 9 * 256
-    out, gw1, gw2 = pl.pallas_call(
-        functools.partial(kernel, count, levels_two, levels_one),
+    size_one, size_two = 9 * 128, 9 * 256
+    out, gw1, gw2, biases = pl.pallas_call(
+        functools.partial(kernel, count, [levels for levels, _ in planned]),
         out_shape=(
             jax.ShapeDtypeStruct(cotangent.shape, BF),
             jax.ShapeDtypeStruct((size_one, 256), BF),
             jax.ShapeDtypeStruct((size_two, 256), BF),
+            jax.ShapeDtypeStruct((16, 256), F32),
         ),
         in_specs=[hbm, hbm, vmem, hbm, vmem, hbm],
-        out_specs=(vmem, vmem, vmem),
+        out_specs=(hbm, hbm, hbm, vmem),
         scratch_shapes=[
+            pltpu.VMEM(cotangent.shape, BF),
             pltpu.VMEM(images.shape, BF),
             pltpu.VMEM(cotangent.shape, BF),
             pltpu.VMEM((9, 128, 256), BF),
@@ -385,32 +433,21 @@
             pltpu.VMEM((rows * cols, 256), F32),
             pltpu.VMEM((rows, 256, cols), BF),
             pltpu.VMEM((rows, 256, cols), BF),
-            pltpu.VMEM((size_two, 256), F32),
-            pltpu.VMEM((span_two, 256), BF),
-            pltpu.VMEM((span_two, 256), BF),
-            pltpu.VMEM((size_two, 256), BF),
-            pltpu.VMEM((size_one, 256), F32),
-            pltpu.VMEM((span_one, 256), BF),
-            pltpu.VMEM((span_one, 256), BF),
-            pltpu.VMEM((size_one, 256), BF),
             pltpu.SemaphoreType.DMA((7,)),
             pltpu.SemaphoreType.DMA((2, 5)),
-            pltpu.SemaphoreType.DMA((2, n)),
-            pltpu.SemaphoreType.DMA((2, n)),
-            pltpu.SemaphoreType.DMA((2, n)),
-            pltpu.SemaphoreType.DMA((2, n)),
+            pltpu.SemaphoreType.DMA((5,)),
+            *stream_shapes,
         ],
         compiler_params=pltpu.CompilerParams(
             collective_id=0, has_side_effects=True, vmem_limit_bytes=56 * 1024 * 1024
         ),
     )(images, weight_one, bias_one[None], weight_two, bias_two[None], cotangent)
-    grads_one = gw1.astype(F32)
     return (
         out,
-        grads_one[:1152].reshape(3, 3, 128, 256),
-        grads_one[1152],
+        gw1.astype(F32).reshape(3, 3, 128, 256),
+        biases[0],
         gw2.astype(F32).reshape(3, 3, 256, 256),
-        grads_one[1216],
+        biases[8],
     )
 
 

time: 70.2 us -> 60.6 us (0.86)
  Pallas kernels: 63.1 us -> 52.8 us
  other arithmetic: 1.63 us -> 4.08 us
  local copies, waits for them, and re-layouts: 4.49 us -> 2.78 us
    pallas_call x1, Pallas kernels: 63.1 us -> 52.8 us  [local(): pl.pallas_call(functools.partial(kernel, count, [levels for levels, _ in...]
    slice x2 -> x1, local copies, waits for them, and re-layouts: 3.51 us -> 1.28 us  [local(): biases[8]]
    reshape x1, other arithmetic: 1.63 us -> 2.96 us  [local(): gw2.astype(F32).reshape(3, 3, 256, 256)]
    reshape x0 -> x1, other arithmetic: none -> 1.12 us  [local(): gw1.astype(F32).reshape(3, 3, 128, 256)]
where the time goes in v1:
time: 60.6 us; the launch traced here: 60.3 us
  Pallas kernels  52.8 us (87%)
  other arithmetic  4.08 us (7%)
  local copies, waits for them, and re-layouts  2.78 us (5%)
  between operations  0.64 us (1%)
    pallas_call x1, Pallas kernels, local(): pl.pallas_call(functools.partial(kernel, count, [levels for levels, _ in...  52.8 us
    reshape x1, other arithmetic, local(): gw2.astype(F32).reshape(3, 3, 256, 256)  2.96 us
    unnamed x5, local copies, waits for them, and re-layouts  1.5 us
    slice x1, local copies, waits for them, and re-layouts, local(): biases[8]  1.28 us

profile of v1, /device:TPU:0, one launch (start us, length us, event | category | flops | bytes accessed | tf_op | source)
XLA Modules:
  0.0 60.3 jit_solution(12139481874426225791)
XLA Ops:
  0.6 52.8 %shard_map.101 = (bf16[8,256,256]{2,1,0:T(8,128)(2,1)}, bf16[1152,256]{1,0:T(8,128)(2,1)}, bf16[2304,256]{1,0:T(8,128)(2,1)}, f32[16,256]{1,0:T(8,128)}) custom-call(bf16[16,512,128]{2,1,0:T(8,128)(2,1)} %img_h.1, bf16[3,3,128,256]{3,2,1,0:T(8,128)(2,1)} %w1_h.1, f32[1,256]{1,0:T(1,128)} %bitcast.10, bf16[3,3,256,256]{3,2,1,0:T(8,128)(2,1)} %w2_h.1, ...), custom_call_target="tpu_custom_call" | custom-call | tf_op jit(solution)/shard_map/pallas_call | solution.py:406
  53.4 1.3 %fusion = (f32[1,256]{1,0:T(1,128)}, f32[1,256]{1,0:T(1,128)}) fusion(f32[16,256]{1,0:T(8,128)} %get-tuple-element.11), kind=kLoop, calls=%fused_computation | loop fusion | bytes 4096 | tf_op jit(solution)/shard_map/slice | solution.py:450
  54.7 0.0 copy-start.1
  54.7 3.0 %convert.3 = f32[3,3,256,256]{3,2,1,0:T(8,128)} convert(bf16[3,3,256,256]{3,2,1,0:T(8,128)(2,1)} %bitcast.8) | non-fusion elementwise | flops 589824 | bytes 3538944 | tf_op jit(solution)/shard_map/reshape | solution.py:449
  57.7 0.0 copy-start
  57.7 0.0 copy-done.1
  57.7 1.1 %convert.2 = f32[3,3,128,256]{3,2,1,0:T(8,128)} convert(bf16[3,3,128,256]{3,2,1,0:T(8,128)(2,1)S(1)} %bitcast.9) | non-fusion elementwise | flops 294912 | bytes 1769472 | tf_op jit(solution)/shard_map/reshape | solution.py:447
  58.8 0.5 copy-done
  59.3 1.0 %copy.12 = bf16[8,256,256]{2,1,0:T(8,128)(2,1)} copy(bf16[8,256,256]{2,1,0:T(8,128)(2,1)S(1)} %copy-done) | data formatting | bytes 2097152
Async XLA Ops:
  54.7 3.0 %copy-start.1 = (bf16[1152,256]{1,0:T(8,128)(2,1)S(1)}, bf16[1152,256]{1,0:T(8,128)(2,1)}, u32[]{:S(2)}) copy-start(bf16[1152,256]{1,0:T(8,128)(2,1)} %get-tuple-element.10) | copy-start | bytes 1769476
  57.7 1.7 %copy-start = (bf16[8,256,256]{2,1,0:T(8,128)(2,1)S(1)}, bf16[8,256,256]{2,1,0:T(8,128)(2,1)}, u32[]{:S(2)}) copy-start(bf16[8,256,256]{2,1,0:T(8,128)(2,1)} %get-tuple-element.20) | copy-start | bytes 3145732

commit v2 on v1

--- a/solution.py
+++ b/solution.py
@@ -29,7 +29,7 @@
     while distance < count:
         near.append(distance)
         distance *= 2
-    return near, near[:1] + near[2:] + near[1:2]
+    return near
 
 
 def remote(src, dst, send, recv, to):
@@ -385,9 +385,9 @@
 
 def local(count, images, weight_one, bias_one, weight_two, bias_two, cotangent):
     rows, cols, depth = cotangent.shape
-    y_first, z_first = order_of(count)
+    y_first = order_of(count)
     totals = (768, 768, 768, 1152, 16)
-    planned = [plan(size, z_first if k == 1 else y_first) for k, size in enumerate(totals)]
+    planned = [plan(size, y_first) for k, size in enumerate(totals)]
     n = len(y_first)
     stream_shapes = []
     for k, (size, (_, span)) in enumerate(zip(totals, planned)):

time: 60.6 us -> 59 us (0.974)
  Pallas kernels: 52.8 us -> 51.2 us
    pallas_call x1, Pallas kernels: 52.8 us -> 51.2 us  [local(): pl.pallas_call(functools.partial(kernel, count, [levels for levels, _ in...]
where the time goes in v2:
time: 59 us; the launch traced here: 58.7 us
  Pallas kernels  51.2 us (87%)
  other arithmetic  4.08 us (7%)
  local copies, waits for them, and re-layouts  2.78 us (5%)
  between operations  0.64 us (1%)
    pallas_call x1, Pallas kernels, local(): pl.pallas_call(functools.partial(kernel, count, [levels for levels, _ in...  51.2 us
    reshape x1, other arithmetic, local(): gw2.astype(F32).reshape(3, 3, 256, 256)  2.96 us
    unnamed x5, local copies, waits for them, and re-layouts  1.5 us
    slice x1, local copies, waits for them, and re-layouts, local(): biases[8]  1.28 us

profile of v2, /device:TPU:0, one launch (start us, length us, event | category | flops | bytes accessed | tf_op | source)
XLA Modules:
  0.0 58.7 jit_solution(14579985265802844773)
XLA Ops:
  0.6 51.2 %shard_map.101 = (bf16[8,256,256]{2,1,0:T(8,128)(2,1)}, bf16[1152,256]{1,0:T(8,128)(2,1)}, bf16[2304,256]{1,0:T(8,128)(2,1)}, f32[16,256]{1,0:T(8,128)}) custom-call(bf16[16,512,128]{2,1,0:T(8,128)(2,1)} %img_h.1, bf16[3,3,128,256]{3,2,1,0:T(8,128)(2,1)} %w1_h.1, f32[1,256]{1,0:T(1,128)} %bitcast.10, bf16[3,3,256,256]{3,2,1,0:T(8,128)(2,1)} %w2_h.1, ...), custom_call_target="tpu_custom_call" | custom-call | tf_op jit(solution)/shard_map/pallas_call | solution.py:406
  51.8 1.3 %fusion = (f32[1,256]{1,0:T(1,128)}, f32[1,256]{1,0:T(1,128)}) fusion(f32[16,256]{1,0:T(8,128)} %get-tuple-element.11), kind=kLoop, calls=%fused_computation | loop fusion | bytes 4096 | tf_op jit(solution)/shard_map/slice | solution.py:450
  53.1 0.0 copy-start.1
  53.1 3.0 %convert.3 = f32[3,3,256,256]{3,2,1,0:T(8,128)} convert(bf16[3,3,256,256]{3,2,1,0:T(8,128)(2,1)} %bitcast.8) | non-fusion elementwise | flops 589824 | bytes 3538944 | tf_op jit(solution)/shard_map/reshape | solution.py:449
  56.1 0.0 copy-start
  56.1 0.0 copy-done.1
  56.1 1.1 %convert.2 = f32[3,3,128,256]{3,2,1,0:T(8,128)} convert(bf16[3,3,128,256]{3,2,1,0:T(8,128)(2,1)S(1)} %bitcast.9) | non-fusion elementwise | flops 294912 | bytes 1769472 | tf_op jit(solution)/shard_map/reshape | solution.py:447
  57.2 0.5 copy-done
  57.7 1.0 %copy.12 = bf16[8,256,256]{2,1,0:T(8,128)(2,1)} copy(bf16[8,256,256]{2,1,0:T(8,128)(2,1)S(1)} %copy-done) | data formatting | bytes 2097152
Async XLA Ops:
  53.1 3.0 %copy-start.1 = (bf16[1152,256]{1,0:T(8,128)(2,1)S(1)}, bf16[1152,256]{1,0:T(8,128)(2,1)}, u32[]{:S(2)}) copy-start(bf16[1152,256]{1,0:T(8,128)(2,1)} %get-tuple-element.10) | copy-start | bytes 1769476
  56.1 1.7 %copy-start = (bf16[8,256,256]{2,1,0:T(8,128)(2,1)S(1)}, bf16[8,256,256]{2,1,0:T(8,128)(2,1)}, u32[]{:S(2)}) copy-start(bf16[8,256,256]{2,1,0:T(8,128)(2,1)} %get-tuple-element.20) | copy-start | bytes 3145732
